TPU v7x, 32 devices: a whole 2x2x4 slice. The times are simulated.
32 devices in a mesh: pipe: 8 (over y, x, core), dp: 4 (over z).
Axes of the slice: x: 2, y: 2, z: 4, core: 2. Of those that a mesh axis runs over, the one named last changes fastest.
Arguments:
- inputs: bfloat16 [4, 384, 3072], P(None, 'dp'), may hold values from -24 to 24
- projection: bfloat16 [8, 3072, 3072], P('pipe'), may hold values from -0.109375 to 0.109375
- cotangent: bfloat16 [4, 384, 3072], P(None, 'dp'), may hold values from -6 to 6
Outputs:
- weight_grad: bfloat16 [8, 3072, 3072], P('pipe', 'dp')
All inputs are finite; a program needn't handle non-finite values.
Results may differ from a plain program's by a relative error of at most 0.033.
Values may be sent and summed in bfloat16 or wider, within the bound.
A program may use at most 192 MiB of HBM per device.

v0:
```python
import math

import jax
import jax.numpy as jnp
from jax import lax
from jax.sharding import PartitionSpec as P

EPSILON = 1e-06


def from_behind(array, axis, by):
    count = lax.axis_size(axis)
    pairs = [(i, i + by) for i in range(count) if 0 <= i + by < count]
    return lax.ppermute(array, axis, pairs)


def norm_factor(values):
    floats = values.astype(jnp.float32)
    factor = lax.rsqrt(jnp.mean(floats * floats, axis=-1, keepdims=True) + EPSILON)
    return (floats, factor)


def forward_layer(values, weight):
    floats, factor = norm_factor(values)
    normed = (floats * factor).astype(jnp.bfloat16)
    gate_value = jnp.dot(normed, weight, preferred_element_type=jnp.float32)
    output = (floats + jax.nn.silu(gate_value)).astype(jnp.bfloat16)
    return (output, gate_value)


def backward_layer(values, gate_value, upstream, weight):
    floats, factor = norm_factor(values)
    up_float = upstream.astype(jnp.float32)
    sigma = jax.nn.sigmoid(gate_value)
    slope = (up_float * sigma * (1.0 + gate_value * (1.0 - sigma))).astype(jnp.bfloat16)
    back = lax.dot_general(
        slope, weight, (((1,), (1,)), ((), ())), preferred_element_type=jnp.float32
    )
    unit = floats * factor
    down = (
        up_float + factor * (back - unit * jnp.mean(back * unit, axis=-1, keepdims=True))
    ).astype(jnp.bfloat16)
    return (down, slope)


def on_device(inputs, projection, cotangent):
    weight = projection[0]
    micro, rows_mb, width = inputs.shape
    section = lax.axis_index("pipe")
    sections = lax.axis_size("pipe")
    replicas = lax.axis_size("dp")
    ticks = micro + sections - 1
    zero_act = jnp.zeros((rows_mb, width), jnp.bfloat16)
    zero_gate = jnp.zeros((rows_mb, width), jnp.float32)

    def run_forward(source):
        return forward_layer(source, weight)

    def skip_forward(source):
        return (zero_act, zero_gate)

    def forward_tick(carry, tick):
        incoming, kept_inputs, kept_gates = carry
        batch = tick - section
        active = (batch >= 0) & (batch < micro)
        slot = jnp.clip(batch, 0, micro - 1)
        first = lax.dynamic_index_in_dim(inputs, slot, 0, keepdims=False)
        source = jnp.where(section == 0, first, incoming)
        output, gate_value = lax.cond(active, run_forward, skip_forward, source)
        old_input = lax.dynamic_index_in_dim(kept_inputs, slot, 0, keepdims=False)
        kept_inputs = lax.dynamic_update_index_in_dim(
            kept_inputs, jnp.where(active, source, old_input), slot, 0
        )
        old_gate = lax.dynamic_index_in_dim(kept_gates, slot, 0, keepdims=False)
        kept_gates = lax.dynamic_update_index_in_dim(
            kept_gates, jnp.where(active, gate_value, old_gate), slot, 0
        )
        incoming = from_behind(output, "pipe", 1)
        return ((incoming, kept_inputs, kept_gates), None)

    start_carry = (
        zero_act,
        jnp.zeros_like(inputs),
        jnp.zeros((micro, rows_mb, width), jnp.float32),
    )
    (unused_act, kept_inputs, kept_gates), unused = lax.scan(
        forward_tick, start_carry, jnp.arange(ticks, dtype=jnp.int32)
    )

    def run_backward(operands):
        source, stored_input, stored_gate = operands
        return backward_layer(stored_input, stored_gate, source, weight)

    def skip_backward(operands):
        return (zero_act, zero_act)

    def backward_tick(carry, tick):
        incoming, kept_slopes = carry
        batch = tick - (sections - 1 - section)
        active = (batch >= 0) & (batch < micro)
        slot = jnp.clip(batch, 0, micro - 1)
        first = lax.dynamic_index_in_dim(cotangent, slot, 0, keepdims=False)
        source = jnp.where(section == sections - 1, first, incoming)
        stored_input = lax.dynamic_index_in_dim(kept_inputs, slot, 0, keepdims=False)
        stored_gate = lax.dynamic_index_in_dim(kept_gates, slot, 0, keepdims=False)
        down, slope = lax.cond(
            active, run_backward, skip_backward, (source, stored_input, stored_gate)
        )
        old_slope = lax.dynamic_index_in_dim(kept_slopes, slot, 0, keepdims=False)
        kept_slopes = lax.dynamic_update_index_in_dim(
            kept_slopes, jnp.where(active, slope, old_slope), slot, 0
        )
        incoming = from_behind(down, "pipe", -1)
        return ((incoming, kept_slopes), None)

    (unused_grad, kept_slopes), unused = lax.scan(
        backward_tick, (zero_act, jnp.zeros_like(cotangent)), jnp.arange(ticks, dtype=jnp.int32)
    )
    shard_rows = micro * rows_mb
    floats, factor = norm_factor(kept_inputs)
    normed_all = (floats * factor).astype(jnp.bfloat16).reshape(shard_rows, width)
    slope_all = kept_slopes.reshape(shard_rows, width)
    summed = lax.psum_scatter(
        lax.dot_general(
            normed_all, slope_all, (((0,), (0,)), ((), ())), preferred_element_type=jnp.float32
        ).astype(jnp.bfloat16),
        "dp",
        scatter_dimension=0,
        tiled=True,
    ).astype(jnp.float32)
    factor_out = 1.0 / math.sqrt(micro * rows_mb * replicas)
    return (summed * factor_out).astype(jnp.bfloat16)[None]


def solution(mesh):
    placed = (P(None, "dp", None), P("pipe", None, None), P(None, "dp", None))
    return jax.shard_map(
        on_device, mesh=mesh, in_specs=placed, out_specs=P("pipe", "dp", None), check_vma=False
    )
```

profile of v0, /device:TPU:0, one launch (start us, length us, event | category | flops | bytes accessed | tf_op | source)
XLA Modules:
  0.0 870.7 jit_solution(3422094577668463073)
XLA Ops:
  6.6 1.7 broadcast.66.clone
  8.3 2.8 broadcast_in_dim.38
  11.1 210.5 %while.29 = (s32[]{:T(128)}, bf16[96,3072]{1,0:T(8,128)(2,1)S(1)}, bf16[4,96,3072]{2,1,0:T(8,128)(2,1)}, f32[4,96,3072]{2,1,0:T(8,128)}, s32[11]{0:T(128)S(1)}, ...) while((s32[]{:T(128)}, bf16[96,3072]{1,0:T(8,128)(2,1)S(1)}, ...), condition=%wide.region_4.5_spmd, body=%wide.region_0.4_spmd.sunk | while | flops 1816658048 | bytes 34212120 | solution.py:86
  13.4 2.2 bitcast_dynamic-update-slice_fusion.6
  15.6 8.4 conditional.4
  15.8 8.2 fusion.2
  30.2 2.2 bitcast_dynamic-update-slice_fusion.6
  32.3 8.4 conditional.4
  32.6 8.2 fusion.2
  40.7 1.6 collective-permute-start
  47.2 2.1 bitcast_dynamic-update-slice_fusion.6
  49.4 8.4 conditional.4
  49.6 8.2 fusion.2
  57.8 6.2 collective-permute-start
  68.8 2.1 bitcast_dynamic-update-slice_fusion.6
  71.0 8.4 conditional.4
  71.2 8.2 fusion.2
  79.4 8.7 collective-permute-start
  92.9 2.1 bitcast_dynamic-update-slice_fusion.6
  95.2 16.9 %collective-permute-start = (bf16[96,3072]{1,0:T(8,128)(2,1)S(1)}, bf16[96,3072]{1,0:T(8,128)(2,1)S(1)}, u32[]{:S(2)}, u32[]{:S(2)}) collective-permute-start(bf16[96,3072]{1,0:T(8,128)(2,1)S(1)} %get-tuple-element.435), channel_id=1, source_target_pairs={{0,4},{4,8},{8,12},{12,16},{16,20},{20,24},{24,28},{1,5},{5,9},{9,... | collective-permute-start | bytes 1769480 | tf_op jit(solution)/shard_map/while/body/eval_jaxpr/ppermute | solution.py:14
  117.0 2.1 bitcast_dynamic-update-slice_fusion.6
  119.3 8.7 collective-permute-start
  132.9 2.1 bitcast_dynamic-update-slice_fusion.6
  135.2 16.9 %collective-permute-start = (bf16[96,3072]{1,0:T(8,128)(2,1)S(1)}, bf16[96,3072]{1,0:T(8,128)(2,1)S(1)}, u32[]{:S(2)}, u32[]{:S(2)}) collective-permute-start(bf16[96,3072]{1,0:T(8,128)(2,1)S(1)} %get-tuple-element.435), channel_id=1, source_target_pairs={{0,4},{4,8},{8,12},{12,16},{16,20},{20,24},{24,28},{1,5},{5,9},{9,... | collective-permute-start | bytes 1769480 | tf_op jit(solution)/shard_map/while/body/eval_jaxpr/ppermute | solution.py:14
  156.9 2.1 bitcast_dynamic-update-slice_fusion.6
  159.3 8.7 collective-permute-start
  172.8 2.1 bitcast_dynamic-update-slice_fusion.6
  175.1 8.7 collective-permute-start
  188.6 2.1 bitcast_dynamic-update-slice_fusion.6
  191.0 8.7 collective-permute-start
  204.5 2.1 bitcast_dynamic-update-slice_fusion.6
  206.8 12.2 %collective-permute-start = (bf16[96,3072]{1,0:T(8,128)(2,1)S(1)}, bf16[96,3072]{1,0:T(8,128)(2,1)S(1)}, u32[]{:S(2)}, u32[]{:S(2)}) collective-permute-start(bf16[96,3072]{1,0:T(8,128)(2,1)S(1)} %get-tuple-element.435), channel_id=1, source_target_pairs={{0,4},{4,8},{8,12},{12,16},{16,20},{20,24},{24,28},{1,5},{5,9},{9,... | collective-permute-start | bytes 1769480 | tf_op jit(solution)/shard_map/while/body/eval_jaxpr/ppermute | solution.py:14
  221.6 2.2 fusion.19
  223.9 1.7 broadcast.66
  225.5 301.7 %while.30 = (s32[]{:T(128)}, bf16[96,3072]{1,0:T(8,128)(2,1)S(1)}, bf16[4,96,3072]{2,1,0:T(8,128)(2,1)}, s32[11]{0:T(128)S(1)}, s32[]{:T(128)}, /*index=5*/pred[...) while((s32[]{:T(128)}, bf16[96,3072]{1,0:T(8,128)(2,1)S(1)}, ...), condition=%wide.region_11.12_spmd, body=%wide.region_6.11_spmd.sunk | while | flops 1820196992 | bytes 38342916 | solution.py:116
  230.3 7.7 collective-permute-done.1
  242.8 9.5 %collective-permute-done.1 = bf16[96,3072]{1,0:T(8,128)(2,1)S(1)} collective-permute-done((bf16[96,3072]{1,0:T(8,128)(2,1)S(1)}, bf16[96,3072]{1,0:T(8,128)(2,1)S(1)}, u32[]{:S(2)}, u32[]{:S(2)}) %collective-permute-start.1) | collective-permute-done | bytes 589856 | tf_op jit(solution)/shard_map/while/body/eval_jaxpr/ppermute | solution.py:14
  257.1 7.8 collective-permute-done.1
  269.7 9.3 %collective-permute-done.1 = bf16[96,3072]{1,0:T(8,128)(2,1)S(1)} collective-permute-done((bf16[96,3072]{1,0:T(8,128)(2,1)S(1)}, bf16[96,3072]{1,0:T(8,128)(2,1)S(1)}, u32[]{:S(2)}, u32[]{:S(2)}) %collective-permute-start.1) | collective-permute-done | bytes 589856 | tf_op jit(solution)/shard_map/while/body/eval_jaxpr/ppermute | solution.py:14
  283.8 8.7 %collective-permute-done.1 = bf16[96,3072]{1,0:T(8,128)(2,1)S(1)} collective-permute-done((bf16[96,3072]{1,0:T(8,128)(2,1)S(1)}, bf16[96,3072]{1,0:T(8,128)(2,1)S(1)}, u32[]{:S(2)}, u32[]{:S(2)}) %collective-permute-start.1) | collective-permute-done | bytes 589856 | tf_op jit(solution)/shard_map/while/body/eval_jaxpr/ppermute | solution.py:14
  297.3 8.7 %collective-permute-done.1 = bf16[96,3072]{1,0:T(8,128)(2,1)S(1)} collective-permute-done((bf16[96,3072]{1,0:T(8,128)(2,1)S(1)}, bf16[96,3072]{1,0:T(8,128)(2,1)S(1)}, u32[]{:S(2)}, u32[]{:S(2)}) %collective-permute-start.1) | collective-permute-done | bytes 589856 | tf_op jit(solution)/shard_map/while/body/eval_jaxpr/ppermute | solution.py:14
  310.9 103.9 %collective-permute-done.1 = bf16[96,3072]{1,0:T(8,128)(2,1)S(1)} collective-permute-done((bf16[96,3072]{1,0:T(8,128)(2,1)S(1)}, bf16[96,3072]{1,0:T(8,128)(2,1)S(1)}, u32[]{:S(2)}, u32[]{:S(2)}) %collective-permute-start.1) | collective-permute-done | bytes 589856 | tf_op jit(solution)/shard_map/while/body/eval_jaxpr/ppermute | solution.py:14
  416.0 16.8 %conditional.5 = (bf16[96,3072]{1,0:T(8,128)(2,1)S(1)}, bf16[96,3072]{1,0:T(8,128)(2,1)S(1)}) conditional(s32[]{:T(128)} %convert_element_type.108, () %tuple.75, (pred[]{:T(512)}, bf16[4,96,3072]{2,1,0:T(8,128)(2,1)}, s32[]{:T(128)}, bf16[96,3072]{1,0:T(8,128)(2,1)S(1)}, bf16[4,96,3072]{2,1,0:T(8,128)(2,1)}, /*index=5*/f32[4,96,3072]{2,1,0:T(8,128)}, ...), branch_computations={%region_7.7_spmd, %region_8.10_spmd} | conditional | flops 1819902080 | bytes 33033684 | solution.py:106
  416.0 2.3 fusion.12
  418.4 12.7 %fusion.8 = (f32[96]{0:T(128)S(1)}, f32[96,3072]{1,0:T(8,128)S(1)}) fusion(f32[96]{0:T(128)S(1)} %add_rsqrt_fusion.1, bf16[4,96,3072]{2,1,0:T(8,128)(2,1)} %get-tuple-element.254, s32[]{:T(128)} %get-tuple-element.252, bf16[96,3072]{1,0:T(8,128)(2,1)S(1)} %get-tuple-element.457, bf16[3072,3072]{1,0:T(8,128)(2,1)} %get-tuple-element.256), kind=kOutput, calls=%fused_computation.22 | convolution fusion | flops 1813118848 | bytes 21234436 | tf_op jit(solution)/shard_map/while/body/eval_jaxpr/cond/branch_1_fun/dot_general | solution.py:36
  431.1 1.7 fusion.13
  436.2 8.7 %collective-permute-done.1 = bf16[96,3072]{1,0:T(8,128)(2,1)S(1)} collective-permute-done((bf16[96,3072]{1,0:T(8,128)(2,1)S(1)}, bf16[96,3072]{1,0:T(8,128)(2,1)S(1)}, u32[]{:S(2)}, u32[]{:S(2)}) %collective-permute-start.1) | collective-permute-done | bytes 589856 | tf_op jit(solution)/shard_map/while/body/eval_jaxpr/ppermute | solution.py:14
  446.2 16.8 %conditional.5 = (bf16[96,3072]{1,0:T(8,128)(2,1)S(1)}, bf16[96,3072]{1,0:T(8,128)(2,1)S(1)}) conditional(s32[]{:T(128)} %convert_element_type.108, () %tuple.75, (pred[]{:T(512)}, bf16[4,96,3072]{2,1,0:T(8,128)(2,1)}, s32[]{:T(128)}, bf16[96,3072]{1,0:T(8,128)(2,1)S(1)}, bf16[4,96,3072]{2,1,0:T(8,128)(2,1)}, /*index=5*/f32[4,96,3072]{2,1,0:T(8,128)}, ...), branch_computations={%region_7.7_spmd, %region_8.10_spmd} | conditional | flops 1819902080 | bytes 33033684 | solution.py:106
  446.2 2.3 fusion.12
  448.5 12.7 %fusion.8 = (f32[96]{0:T(128)S(1)}, f32[96,3072]{1,0:T(8,128)S(1)}) fusion(f32[96]{0:T(128)S(1)} %add_rsqrt_fusion.1, bf16[4,96,3072]{2,1,0:T(8,128)(2,1)} %get-tuple-element.254, s32[]{:T(128)} %get-tuple-element.252, bf16[96,3072]{1,0:T(8,128)(2,1)S(1)} %get-tuple-element.457, bf16[3072,3072]{1,0:T(8,128)(2,1)} %get-tuple-element.256), kind=kOutput, calls=%fused_computation.22 | convolution fusion | flops 1813118848 | bytes 21234436 | tf_op jit(solution)/shard_map/while/body/eval_jaxpr/cond/branch_1_fun/dot_general | solution.py:36
  461.2 1.7 fusion.13
  466.3 8.7 %collective-permute-done.1 = bf16[96,3072]{1,0:T(8,128)(2,1)S(1)} collective-permute-done((bf16[96,3072]{1,0:T(8,128)(2,1)S(1)}, bf16[96,3072]{1,0:T(8,128)(2,1)S(1)}, u32[]{:S(2)}, u32[]{:S(2)}) %collective-permute-start.1) | collective-permute-done | bytes 589856 | tf_op jit(solution)/shard_map/while/body/eval_jaxpr/ppermute | solution.py:14
  476.4 16.8 %conditional.5 = (bf16[96,3072]{1,0:T(8,128)(2,1)S(1)}, bf16[96,3072]{1,0:T(8,128)(2,1)S(1)}) conditional(s32[]{:T(128)} %convert_element_type.108, () %tuple.75, (pred[]{:T(512)}, bf16[4,96,3072]{2,1,0:T(8,128)(2,1)}, s32[]{:T(128)}, bf16[96,3072]{1,0:T(8,128)(2,1)S(1)}, bf16[4,96,3072]{2,1,0:T(8,128)(2,1)}, /*index=5*/f32[4,96,3072]{2,1,0:T(8,128)}, ...), branch_computations={%region_7.7_spmd, %region_8.10_spmd} | conditional | flops 1819902080 | bytes 33033684 | solution.py:106
  476.4 2.3 fusion.12
  478.7 12.7 %fusion.8 = (f32[96]{0:T(128)S(1)}, f32[96,3072]{1,0:T(8,128)S(1)}) fusion(f32[96]{0:T(128)S(1)} %add_rsqrt_fusion.1, bf16[4,96,3072]{2,1,0:T(8,128)(2,1)} %get-tuple-element.254, s32[]{:T(128)} %get-tuple-element.252, bf16[96,3072]{1,0:T(8,128)(2,1)S(1)} %get-tuple-element.457, bf16[3072,3072]{1,0:T(8,128)(2,1)} %get-tuple-element.256), kind=kOutput, calls=%fused_computation.22 | convolution fusion | flops 1813118848 | bytes 21234436 | tf_op jit(solution)/shard_map/while/body/eval_jaxpr/cond/branch_1_fun/dot_general | solution.py:36
  491.4 1.7 fusion.13
  496.5 8.7 %collective-permute-done.1 = bf16[96,3072]{1,0:T(8,128)(2,1)S(1)} collective-permute-done((bf16[96,3072]{1,0:T(8,128)(2,1)S(1)}, bf16[96,3072]{1,0:T(8,128)(2,1)S(1)}, u32[]{:S(2)}, u32[]{:S(2)}) %collective-permute-start.1) | collective-permute-done | bytes 589856 | tf_op jit(solution)/shard_map/while/body/eval_jaxpr/ppermute | solution.py:14
  506.5 16.8 %conditional.5 = (bf16[96,3072]{1,0:T(8,128)(2,1)S(1)}, bf16[96,3072]{1,0:T(8,128)(2,1)S(1)}) conditional(s32[]{:T(128)} %convert_element_type.108, () %tuple.75, (pred[]{:T(512)}, bf16[4,96,3072]{2,1,0:T(8,128)(2,1)}, s32[]{:T(128)}, bf16[96,3072]{1,0:T(8,128)(2,1)S(1)}, bf16[4,96,3072]{2,1,0:T(8,128)(2,1)}, /*index=5*/f32[4,96,3072]{2,1,0:T(8,128)}, ...), branch_computations={%region_7.7_spmd, %region_8.10_spmd} | conditional | flops 1819902080 | bytes 33033684 | solution.py:106
  506.6 2.3 fusion.12
  508.9 12.7 %fusion.8 = (f32[96]{0:T(128)S(1)}, f32[96,3072]{1,0:T(8,128)S(1)}) fusion(f32[96]{0:T(128)S(1)} %add_rsqrt_fusion.1, bf16[4,96,3072]{2,1,0:T(8,128)(2,1)} %get-tuple-element.254, s32[]{:T(128)} %get-tuple-element.252, bf16[96,3072]{1,0:T(8,128)(2,1)S(1)} %get-tuple-element.457, bf16[3072,3072]{1,0:T(8,128)(2,1)} %get-tuple-element.256), kind=kOutput, calls=%fused_computation.22 | convolution fusion | flops 1813118848 | bytes 21234436 | tf_op jit(solution)/shard_map/while/body/eval_jaxpr/cond/branch_1_fun/dot_general | solution.py:36
  521.6 1.7 fusion.13
  527.2 16.1 %bitcast_convert_fusion = bf16[3072,3072]{1,0:T(8,128)(2,1)} fusion(bf16[4,96,3072]{2,1,0:T(8,128)(2,1)} %get-tuple-element.275, bf16[4,96,3072]{2,1,0:T(8,128)(2,1)} %get-tuple-element.504, f32[4,96]{1,0:T(4,128)S(1)} %add_rsqrt_fusion.2), kind=kOutput, calls=%fused_computation.41 | convolution fusion | flops 7260733440 | bytes 23594496 | tf_op jit(solution)/shard_map/dot_general | solution.py:124
  543.3 314.8 %reduce-scatter.2.cloned.1.call-done = bf16[768,3072]{1,0:T(8,128)(2,1)} async-done(((bf16[3072,3072]{1,0:T(8,128)(2,1)}), bf16[768,3072]{1,0:T(8,128)(2,1)}) %reduce-scatter.2.cloned.1.call-update) | async-done | bytes 4718608 | tf_op jit(solution)/shard_map/reduce_scatter | solution.py:123
  858.1 5.7 fusion.21
  (182 shorter events, 97.1 us)
Async XLA Ops:
  6.5 851.6 %reduce-scatter.2.cloned.1.call-start = ((), (), s32[]{:S(2)}) async-start(), calls=%async_computation.1 | async-start | bytes 23592960 | tf_op jit(solution)/shard_map/reduce_scatter | solution.py:123
  24.0 3.9 collective-permute-start
  40.7 4.2 collective-permute-start
  57.8 8.7 %collective-permute-start = (bf16[96,3072]{1,0:T(8,128)(2,1)S(1)}, bf16[96,3072]{1,0:T(8,128)(2,1)S(1)}, u32[]{:S(2)}, u32[]{:S(2)}) collective-permute-start(bf16[96,3072]{1,0:T(8,128)(2,1)S(1)} %get-tuple-element.435), channel_id=1, source_target_pairs={{0,4},{4,8},{8,12},{12,16},{16,20},{20,24},{24,28},{1,5},{5,9},{9,... | collective-permute-start | bytes 1769480 | tf_op jit(solution)/shard_map/while/body/eval_jaxpr/ppermute | solution.py:14
  79.4 11.2 %collective-permute-start = (bf16[96,3072]{1,0:T(8,128)(2,1)S(1)}, bf16[96,3072]{1,0:T(8,128)(2,1)S(1)}, u32[]{:S(2)}, u32[]{:S(2)}) collective-permute-start(bf16[96,3072]{1,0:T(8,128)(2,1)S(1)} %get-tuple-element.435), channel_id=1, source_target_pairs={{0,4},{4,8},{8,12},{12,16},{16,20},{20,24},{24,28},{1,5},{5,9},{9,... | collective-permute-start | bytes 1769480 | tf_op jit(solution)/shard_map/while/body/eval_jaxpr/ppermute | solution.py:14
  95.2 19.4 %collective-permute-start = (bf16[96,3072]{1,0:T(8,128)(2,1)S(1)}, bf16[96,3072]{1,0:T(8,128)(2,1)S(1)}, u32[]{:S(2)}, u32[]{:S(2)}) collective-permute-start(bf16[96,3072]{1,0:T(8,128)(2,1)S(1)} %get-tuple-element.435), channel_id=1, source_target_pairs={{0,4},{4,8},{8,12},{12,16},{16,20},{20,24},{24,28},{1,5},{5,9},{9,... | collective-permute-start | bytes 1769480 | tf_op jit(solution)/shard_map/while/body/eval_jaxpr/ppermute | solution.py:14
  119.3 11.2 %collective-permute-start = (bf16[96,3072]{1,0:T(8,128)(2,1)S(1)}, bf16[96,3072]{1,0:T(8,128)(2,1)S(1)}, u32[]{:S(2)}, u32[]{:S(2)}) collective-permute-start(bf16[96,3072]{1,0:T(8,128)(2,1)S(1)} %get-tuple-element.435), channel_id=1, source_target_pairs={{0,4},{4,8},{8,12},{12,16},{16,20},{20,24},{24,28},{1,5},{5,9},{9,... | collective-permute-start | bytes 1769480 | tf_op jit(solution)/shard_map/while/body/eval_jaxpr/ppermute | solution.py:14
  135.2 19.4 %collective-permute-start = (bf16[96,3072]{1,0:T(8,128)(2,1)S(1)}, bf16[96,3072]{1,0:T(8,128)(2,1)S(1)}, u32[]{:S(2)}, u32[]{:S(2)}) collective-permute-start(bf16[96,3072]{1,0:T(8,128)(2,1)S(1)} %get-tuple-element.435), channel_id=1, source_target_pairs={{0,4},{4,8},{8,12},{12,16},{16,20},{20,24},{24,28},{1,5},{5,9},{9,... | collective-permute-start | bytes 1769480 | tf_op jit(solution)/shard_map/while/body/eval_jaxpr/ppermute | solution.py:14
  159.3 11.2 %collective-permute-start = (bf16[96,3072]{1,0:T(8,128)(2,1)S(1)}, bf16[96,3072]{1,0:T(8,128)(2,1)S(1)}, u32[]{:S(2)}, u32[]{:S(2)}) collective-permute-start(bf16[96,3072]{1,0:T(8,128)(2,1)S(1)} %get-tuple-element.435), channel_id=1, source_target_pairs={{0,4},{4,8},{8,12},{12,16},{16,20},{20,24},{24,28},{1,5},{5,9},{9,... | collective-permute-start | bytes 1769480 | tf_op jit(solution)/shard_map/while/body/eval_jaxpr/ppermute | solution.py:14
  175.1 11.2 %collective-permute-start = (bf16[96,3072]{1,0:T(8,128)(2,1)S(1)}, bf16[96,3072]{1,0:T(8,128)(2,1)S(1)}, u32[]{:S(2)}, u32[]{:S(2)}) collective-permute-start(bf16[96,3072]{1,0:T(8,128)(2,1)S(1)} %get-tuple-element.435), channel_id=1, source_target_pairs={{0,4},{4,8},{8,12},{12,16},{16,20},{20,24},{24,28},{1,5},{5,9},{9,... | collective-permute-start | bytes 1769480 | tf_op jit(solution)/shard_map/while/body/eval_jaxpr/ppermute | solution.py:14
  191.0 11.2 %collective-permute-start = (bf16[96,3072]{1,0:T(8,128)(2,1)S(1)}, bf16[96,3072]{1,0:T(8,128)(2,1)S(1)}, u32[]{:S(2)}, u32[]{:S(2)}) collective-permute-start(bf16[96,3072]{1,0:T(8,128)(2,1)S(1)} %get-tuple-element.435), channel_id=1, source_target_pairs={{0,4},{4,8},{8,12},{12,16},{16,20},{20,24},{24,28},{1,5},{5,9},{9,... | collective-permute-start | bytes 1769480 | tf_op jit(solution)/shard_map/while/body/eval_jaxpr/ppermute | solution.py:14
  206.8 14.8 %collective-permute-start = (bf16[96,3072]{1,0:T(8,128)(2,1)S(1)}, bf16[96,3072]{1,0:T(8,128)(2,1)S(1)}, u32[]{:S(2)}, u32[]{:S(2)}) collective-permute-start(bf16[96,3072]{1,0:T(8,128)(2,1)S(1)} %get-tuple-element.435), channel_id=1, source_target_pairs={{0,4},{4,8},{8,12},{12,16},{16,20},{20,24},{24,28},{1,5},{5,9},{9,... | collective-permute-start | bytes 1769480 | tf_op jit(solution)/shard_map/while/body/eval_jaxpr/ppermute | solution.py:14
  227.0 11.0 %collective-permute-start.1 = (bf16[96,3072]{1,0:T(8,128)(2,1)S(1)}, bf16[96,3072]{1,0:T(8,128)(2,1)S(1)}, u32[]{:S(2)}, u32[]{:S(2)}) collective-permute-start(bf16[96,3072]{1,0:T(8,128)(2,1)S(1)} %get-tuple-element.448), channel_id=1, source_target_pairs={{4,0},{8,4},{12,8},{16,12},{20,16},{24,20},{28,24},{5,1},{9,5},{13... | collective-permute-start | bytes 1769480 | tf_op jit(solution)/shard_map/while/body/eval_jaxpr/ppermute | solution.py:14
  239.4 12.8 %collective-permute-start.1 = (bf16[96,3072]{1,0:T(8,128)(2,1)S(1)}, bf16[96,3072]{1,0:T(8,128)(2,1)S(1)}, u32[]{:S(2)}, u32[]{:S(2)}) collective-permute-start(bf16[96,3072]{1,0:T(8,128)(2,1)S(1)} %get-tuple-element.448), channel_id=1, source_target_pairs={{4,0},{8,4},{12,8},{16,12},{20,16},{24,20},{28,24},{5,1},{9,5},{13... | collective-permute-start | bytes 1769480 | tf_op jit(solution)/shard_map/while/body/eval_jaxpr/ppermute | solution.py:14
  253.7 11.2 %collective-permute-start.1 = (bf16[96,3072]{1,0:T(8,128)(2,1)S(1)}, bf16[96,3072]{1,0:T(8,128)(2,1)S(1)}, u32[]{:S(2)}, u32[]{:S(2)}) collective-permute-start(bf16[96,3072]{1,0:T(8,128)(2,1)S(1)} %get-tuple-element.448), channel_id=1, source_target_pairs={{4,0},{8,4},{12,8},{16,12},{20,16},{24,20},{28,24},{5,1},{9,5},{13... | collective-permute-start | bytes 1769480 | tf_op jit(solution)/shard_map/while/body/eval_jaxpr/ppermute | solution.py:14
  266.3 12.7 %collective-permute-start.1 = (bf16[96,3072]{1,0:T(8,128)(2,1)S(1)}, bf16[96,3072]{1,0:T(8,128)(2,1)S(1)}, u32[]{:S(2)}, u32[]{:S(2)}) collective-permute-start(bf16[96,3072]{1,0:T(8,128)(2,1)S(1)} %get-tuple-element.448), channel_id=1, source_target_pairs={{4,0},{8,4},{12,8},{16,12},{20,16},{24,20},{28,24},{5,1},{9,5},{13... | collective-permute-start | bytes 1769480 | tf_op jit(solution)/shard_map/while/body/eval_jaxpr/ppermute | solution.py:14
  280.4 12.1 %collective-permute-start.1 = (bf16[96,3072]{1,0:T(8,128)(2,1)S(1)}, bf16[96,3072]{1,0:T(8,128)(2,1)S(1)}, u32[]{:S(2)}, u32[]{:S(2)}) collective-permute-start(bf16[96,3072]{1,0:T(8,128)(2,1)S(1)} %get-tuple-element.448), channel_id=1, source_target_pairs={{4,0},{8,4},{12,8},{16,12},{20,16},{24,20},{28,24},{5,1},{9,5},{13... | collective-permute-start | bytes 1769480 | tf_op jit(solution)/shard_map/while/body/eval_jaxpr/ppermute | solution.py:14
  294.0 12.1 %collective-permute-start.1 = (bf16[96,3072]{1,0:T(8,128)(2,1)S(1)}, bf16[96,3072]{1,0:T(8,128)(2,1)S(1)}, u32[]{:S(2)}, u32[]{:S(2)}) collective-permute-start(bf16[96,3072]{1,0:T(8,128)(2,1)S(1)} %get-tuple-element.448), channel_id=1, source_target_pairs={{4,0},{8,4},{12,8},{16,12},{20,16},{24,20},{28,24},{5,1},{9,5},{13... | collective-permute-start | bytes 1769480 | tf_op jit(solution)/shard_map/while/body/eval_jaxpr/ppermute | solution.py:14
  307.5 107.2 %collective-permute-start.1 = (bf16[96,3072]{1,0:T(8,128)(2,1)S(1)}, bf16[96,3072]{1,0:T(8,128)(2,1)S(1)}, u32[]{:S(2)}, u32[]{:S(2)}) collective-permute-start(bf16[96,3072]{1,0:T(8,128)(2,1)S(1)} %get-tuple-element.448), channel_id=1, source_target_pairs={{4,0},{8,4},{12,8},{16,12},{20,16},{24,20},{28,24},{5,1},{9,5},{13... | collective-permute-start | bytes 1769480 | tf_op jit(solution)/shard_map/while/body/eval_jaxpr/ppermute | solution.py:14
  418.3 12.7 %copy-start = (bf16[96,3072]{1,0:T(8,128)(2,1)}, bf16[96,3072]{1,0:T(8,128)(2,1)S(1)}, u32[]{:S(2)}) copy-start(bf16[96,3072]{1,0:T(8,128)(2,1)S(1)} %get-tuple-element.457) | copy-start | bytes 1769476 | tf_op jit(solution)/shard_map/while/body/eval_jaxpr/cond
  431.0 1.7 copy-start.1
  432.8 12.1 %collective-permute-start.1 = (bf16[96,3072]{1,0:T(8,128)(2,1)S(1)}, bf16[96,3072]{1,0:T(8,128)(2,1)S(1)}, u32[]{:S(2)}, u32[]{:S(2)}) collective-permute-start(bf16[96,3072]{1,0:T(8,128)(2,1)S(1)} %get-tuple-element.448), channel_id=1, source_target_pairs={{4,0},{8,4},{12,8},{16,12},{20,16},{24,20},{28,24},{5,1},{9,5},{13... | collective-permute-start | bytes 1769480 | tf_op jit(solution)/shard_map/while/body/eval_jaxpr/ppermute | solution.py:14
  448.5 12.7 %copy-start = (bf16[96,3072]{1,0:T(8,128)(2,1)}, bf16[96,3072]{1,0:T(8,128)(2,1)S(1)}, u32[]{:S(2)}) copy-start(bf16[96,3072]{1,0:T(8,128)(2,1)S(1)} %get-tuple-element.457) | copy-start | bytes 1769476 | tf_op jit(solution)/shard_map/while/body/eval_jaxpr/cond
  461.2 1.7 copy-start.1
  463.0 12.1 %collective-permute-start.1 = (bf16[96,3072]{1,0:T(8,128)(2,1)S(1)}, bf16[96,3072]{1,0:T(8,128)(2,1)S(1)}, u32[]{:S(2)}, u32[]{:S(2)}) collective-permute-start(bf16[96,3072]{1,0:T(8,128)(2,1)S(1)} %get-tuple-element.448), channel_id=1, source_target_pairs={{4,0},{8,4},{12,8},{16,12},{20,16},{24,20},{28,24},{5,1},{9,5},{13... | collective-permute-start | bytes 1769480 | tf_op jit(solution)/shard_map/while/body/eval_jaxpr/ppermute | solution.py:14
  478.7 12.7 %copy-start = (bf16[96,3072]{1,0:T(8,128)(2,1)}, bf16[96,3072]{1,0:T(8,128)(2,1)S(1)}, u32[]{:S(2)}) copy-start(bf16[96,3072]{1,0:T(8,128)(2,1)S(1)} %get-tuple-element.457) | copy-start | bytes 1769476 | tf_op jit(solution)/shard_map/while/body/eval_jaxpr/cond
  491.4 1.7 copy-start.1
  493.1 12.1 %collective-permute-start.1 = (bf16[96,3072]{1,0:T(8,128)(2,1)S(1)}, bf16[96,3072]{1,0:T(8,128)(2,1)S(1)}, u32[]{:S(2)}, u32[]{:S(2)}) collective-permute-start(bf16[96,3072]{1,0:T(8,128)(2,1)S(1)} %get-tuple-element.448), channel_id=1, source_target_pairs={{4,0},{8,4},{12,8},{16,12},{20,16},{24,20},{28,24},{5,1},{9,5},{13... | collective-permute-start | bytes 1769480 | tf_op jit(solution)/shard_map/while/body/eval_jaxpr/ppermute | solution.py:14
  508.9 12.7 %copy-start = (bf16[96,3072]{1,0:T(8,128)(2,1)}, bf16[96,3072]{1,0:T(8,128)(2,1)S(1)}, u32[]{:S(2)}) copy-start(bf16[96,3072]{1,0:T(8,128)(2,1)S(1)} %get-tuple-element.457) | copy-start | bytes 1769476 | tf_op jit(solution)/shard_map/while/body/eval_jaxpr/cond
  521.6 1.7 copy-start.1
  523.3 3.9 collective-permute-start.1
Sparse Core Ops, SparseCore 0:
  543.5 314.5 reduce-scatter.1
where the time goes:
time: 874 us; the launch traced here: 871 us
  waiting for transfers between devices  497 us (57%)
  starting transfers between devices  113 us (13%)
  matrix products  99.5 us (11%)
  other arithmetic  71.9 us (8%)
  local copies, waits for them, and re-layouts  60.8 us (7%)
  loops' own time  15.2 us (2%)
  between operations  13.4 us (2%)
    reduce_scatter x1, waiting for transfers between devices, on_device(): lax.psum_scatter(lax.dot_general(normed_all, slope_all, (((0,), (0,)), ((...  315 us
    ppermute x22, waiting for transfers between devices, from_behind(): return lax.ppermute(array, axis, pairs)  182 us
    ppermute x22, starting transfers between devices, from_behind(): return lax.ppermute(array, axis, pairs)  113 us
    dot_general x4, matrix products, backward_layer(): lax.dot_general(slope, weight, (((1,), (1,)), ((), ())), preferred_elemen...  50.7 us
    dot_general x4, matrix products, forward_layer(): gate_value = jnp.dot(normed, weight, preferred_element_type=jnp.float32)  32.7 us
    dynamic_update_slice x11, other arithmetic, forward_tick(): lax.dynamic_update_index_in_dim(kept_inputs, jnp.where(active, source, ol...  23.6 us
  transfers between devices with their start and end apart: 23, of which 12 were waited for; matrix products, arithmetic and copies ran while one was open for 6% of the time, Pallas kernels for 0%

commit v1 on v0

v1 whole, which is shorter than its diff:
```python
import functools
import math

import jax
import jax.numpy as jnp
from jax import lax
from jax.experimental import pallas as pl
from jax.experimental.pallas import tpu as pltpu
from jax.sharding import PartitionSpec as P

EPSILON = 1e-06
TILE = 512
OUT_TILE = 256


def relay_kernel(
    micro, sections, replicas,
    in_ref, w_hbm, cot_ref, out_ref,
    w, xs, acts, gates, ups, slopes, normed, normed_in, normed_t, facs,
    w_sem, first_sem, cot_sem, act_send, act_recv, down_send, down_recv,
    norm_send, norm_recv, right_send, left_send, slope_recv,
):
    section = lax.axis_index("pipe")
    me = lax.axis_index("dp")
    tokens, width = xs.shape
    rows = tokens // micro
    chunk = width // replicas
    tiles = width // TILE
    is_first = section == 0
    is_last = section == sections - 1
    after = lax.rem(section + 1, sections)
    before = lax.rem(section + sections - 1, sections)

    def rows_of(m):
        return pl.ds(pl.multiple_of(m * rows, rows), rows)

    def cols_of(n):
        return pl.ds(pl.multiple_of(n * TILE, TILE), TILE)

    load_w = pltpu.make_async_copy(w_hbm, w, w_sem)
    load_w.start()

    def load_first(m):
        return pltpu.make_async_copy(in_ref.at[rows_of(m)], xs.at[rows_of(m)], first_sem.at[m])

    def load_cot(m):
        return pltpu.make_async_copy(cot_ref.at[rows_of(m)], ups.at[rows_of(m)], cot_sem.at[m])

    @pl.when(is_first)
    def _():
        @pl.loop(0, micro)
        def _(m):
            load_first(m).start()

    @pl.when(is_last)
    def _():
        @pl.loop(0, micro)
        def _(m):
            load_cot(m).start()

    barrier = pltpu.get_barrier_semaphore()
    for other in (after, before):
        pl.semaphore_signal(barrier, inc=1, device_id={"pipe": other})
    for step in range(1, replicas):
        peer = lax.rem(me + step, replicas)
        pl.semaphore_signal(barrier, inc=1, device_id={"dp": peer})
    pl.semaphore_wait(barrier, 2 + replicas - 1)
    load_w.wait()

    def act_copy(m, cols=None):
        where = (rows_of(m),) if cols is None else (rows_of(m), cols)
        return pltpu.make_async_remote_copy(
            src_ref=acts.at[where], dst_ref=xs.at[where],
            send_sem=act_send.at[m], recv_sem=act_recv.at[m], device_id={"pipe": after},
        )

    def down_copy(m, cols=None):
        where = (rows_of(m),) if cols is None else (rows_of(m), cols)
        return pltpu.make_async_remote_copy(
            src_ref=acts.at[where], dst_ref=ups.at[where],
            send_sem=down_send.at[m], recv_sem=down_recv.at[m], device_id={"pipe": before},
        )

    def norm_copy(m, step):
        peer = lax.rem(me + step, replicas)
        cols = pl.ds(pl.multiple_of(peer * chunk, chunk), chunk)
        return pltpu.make_async_remote_copy(
            src_ref=normed.at[rows_of(m), cols], dst_ref=normed_in.at[me, rows_of(m)],
            send_sem=norm_send.at[step, m], recv_sem=norm_recv.at[step, m],
            device_id={"dp": peer},
        )

    def norm_arrival(m, step):
        origin = lax.rem(me + replicas - step, replicas)
        return pltpu.make_async_remote_copy(
            src_ref=normed.at[rows_of(m), pl.ds(0, chunk)],
            dst_ref=normed_in.at[origin, rows_of(m)],
            send_sem=norm_send.at[step, m], recv_sem=norm_recv.at[step, m],
            device_id={"dp": origin},
        )

    def slope_copy(origin, m, to, sends):
        block = slopes.at[origin, rows_of(m)]
        return pltpu.make_async_remote_copy(
            src_ref=block, dst_ref=block,
            send_sem=sends.at[origin, m], recv_sem=slope_recv.at[origin, m],
            device_id={"dp": to},
        )

    def go_right(origin, m):
        return slope_copy(origin, m, me + 1, right_send)

    def go_left(origin, m):
        return slope_copy(origin, m, me - 1, left_send)

    @pl.loop(0, micro)
    def _(m):
        here = rows_of(m)

        @pl.when(is_first)
        def _():
            load_first(m).wait()

        @pl.when(jnp.logical_not(is_first))
        def _():
            act_copy(m).wait_recv()

        def squares(n, total):
            part = xs[here, cols_of(n)].astype(jnp.float32)
            return total + jnp.sum(part * part, axis=-1, keepdims=True)

        total = lax.fori_loop(0, tiles, squares, jnp.zeros((rows, 1), jnp.float32))
        fac = lax.rsqrt(total / width + EPSILON)
        facs[here, :] = jnp.broadcast_to(fac, (rows, 128))

        @pl.loop(0, tiles)
        def _(n):
            part = xs[here, cols_of(n)].astype(jnp.float32)
            normed[here, cols_of(n)] = (part * fac).astype(jnp.bfloat16)

        for step in range(1, replicas):
            norm_copy(m, step).start()

        @pl.loop(0, tiles)
        def _(n):
            cols = cols_of(n)
            gate = jnp.dot(normed[here, :], w[:, cols], preferred_element_type=jnp.float32)
            gates[here, cols] = gate
            out = xs[here, cols].astype(jnp.float32) + gate / (1.0 + jnp.exp(-gate))
            acts[here, cols] = out.astype(jnp.bfloat16)

            @pl.when(jnp.logical_not(is_last))
            def _():
                act_copy(m, cols).start()

    @pl.when(jnp.logical_not(is_last))
    def _():
        @pl.loop(0, micro)
        def _(m):
            act_copy(m).wait_send()

    @pl.loop(0, micro)
    def _(m):
        here = rows_of(m)

        @pl.when(is_last)
        def _():
            load_cot(m).wait()

        @pl.when(jnp.logical_not(is_last))
        def _():
            down_copy(m).wait_recv()

        @pl.loop(0, tiles)
        def _(n):
            cols = cols_of(n)
            gate = gates[here, cols]
            sig = 1.0 / (1.0 + jnp.exp(-gate))
            up = ups[here, cols].astype(jnp.float32)
            slope = up * sig * (1.0 + gate * (1.0 - sig))
            slopes[me, here, cols] = slope.astype(jnp.bfloat16)

        @pl.when(me < replicas - 1)
        def _():
            go_right(me, m).start()

        @pl.when(me > 0)
        def _():
            go_left(me, m).start()

        fac = facs[here, pl.ds(0, 1)]

        @pl.when(jnp.logical_not(is_first))
        def _():
            def back_tile(n, total):
                cols = cols_of(n)
                back = lax.dot_general(
                    slopes[me, here, :], w[cols, :], (((1,), (1,)), ((), ())),
                    preferred_element_type=jnp.float32,
                )
                gates[here, cols] = back
                unit = xs[here, cols].astype(jnp.float32) * fac
                return total + jnp.sum(back * unit, axis=-1, keepdims=True)

            total = lax.fori_loop(0, tiles, back_tile, jnp.zeros((rows, 1), jnp.float32))
            mean = total / width

            @pl.loop(0, tiles)
            def _(n):
                cols = cols_of(n)
                unit = xs[here, cols].astype(jnp.float32) * fac
                down = ups[here, cols].astype(jnp.float32) + fac * (gates[here, cols] - unit * mean)
                acts[here, cols] = down.astype(jnp.bfloat16)
                down_copy(m, cols).start()

    for step in range(1, replicas):
        @pl.loop(0, micro)
        def _(m):
            norm_arrival(m, step).wait_recv()

    own = pl.ds(pl.multiple_of(me * chunk, chunk), chunk)
    normed_in[me] = normed[:, own]
    for origin in range(replicas):
        normed_t[:, pl.ds(origin * tokens, tokens)] = normed_in[origin].T

    for far in range(1, replicas):
        @pl.loop(0, micro)
        def _(m):
            @pl.when(me - far >= 0)
            def _():
                go_right(me - far, m).wait_recv()

                @pl.when(me < replicas - 1)
                def _():
                    go_right(me - far, m).start()

            @pl.when(me + far < replicas)
            def _():
                go_left(me + far, m).wait_recv()

                @pl.when(me > 0)
                def _():
                    go_left(me + far, m).start()

    scale = 1.0 / math.sqrt(tokens * replicas)

    @pl.loop(0, width // OUT_TILE)
    def _(n):
        cols = pl.ds(pl.multiple_of(n * OUT_TILE, OUT_TILE), OUT_TILE)
        right = slopes[:, :, cols].reshape(replicas * tokens, OUT_TILE)
        total = jnp.dot(normed_t[...], right, preferred_element_type=jnp.float32)
        out_ref[:, cols] = (total * scale).astype(jnp.bfloat16)

    @pl.loop(0, micro)
    def _(m):
        for step in range(1, replicas):
            norm_copy(m, step).wait_send()

        @pl.when(jnp.logical_not(is_first))
        def _():
            down_copy(m).wait_send()

        for origin in range(replicas):
            @pl.when(jnp.logical_and(me >= origin, me < replicas - 1))
            def _():
                go_right(origin, m).wait_send()

            @pl.when(jnp.logical_and(me <= origin, me > 0))
            def _():
                go_left(origin, m).wait_send()


def on_device(sections, replicas, inputs, projection, cotangent):
    micro, rows, width = inputs.shape
    tokens = micro * rows
    chunk = width // replicas
    bf16, f32 = jnp.bfloat16, jnp.float32
    dma = pltpu.SemaphoreType.DMA
    out = pl.pallas_call(
        functools.partial(relay_kernel, micro, sections, replicas),
        out_shape=jax.ShapeDtypeStruct((chunk, width), bf16),
        in_specs=[pl.BlockSpec(memory_space=pl.ANY)] * 3,
        out_specs=pl.BlockSpec(memory_space=pltpu.VMEM),
        scratch_shapes=[
            pltpu.VMEM((width, width), bf16),
            pltpu.VMEM((tokens, width), bf16),
            pltpu.VMEM((tokens, width), bf16),
            pltpu.VMEM((tokens, width), f32),
            pltpu.VMEM((tokens, width), bf16),
            pltpu.VMEM((replicas, tokens, width), bf16),
            pltpu.VMEM((tokens, width), bf16),
            pltpu.VMEM((replicas, tokens, chunk), bf16),
            pltpu.VMEM((chunk, replicas * tokens), bf16),
            pltpu.VMEM((tokens, 128), f32),
            dma, dma((micro,)), dma((micro,)),
            dma((micro,)), dma((micro,)), dma((micro,)), dma((micro,)),
            dma((replicas, micro)), dma((replicas, micro)),
            dma((replicas, micro)), dma((replicas, micro)), dma((replicas, micro)),
        ],
        compiler_params=pltpu.CompilerParams(
            collective_id=0, has_side_effects=True, vmem_limit_bytes=64 * 1024 * 1024
        ),
        cost_estimate=pl.CostEstimate(
            flops=6 * tokens * width * width,
            bytes_accessed=2 * width * (width + 2 * tokens + chunk),
            transcendentals=2 * tokens * width,
        ),
    )(inputs.reshape(tokens, width), projection[0], cotangent.reshape(tokens, width))
    return out[None]


def solution(mesh):
    placed = (P(None, "dp", None), P("pipe", None, None), P(None, "dp", None))
    body = functools.partial(on_device, mesh.shape["pipe"], mesh.shape["dp"])
    return jax.shard_map(
        body, mesh=mesh, in_specs=placed, out_specs=P("pipe", "dp", None), check_vma=False
    )
```

time: 874 us -> 338 us (0.39)
  waiting for transfers between devices: 497 us -> 0 us
  Pallas kernels: 0 us -> 333 us
  starting transfers between devices: 113 us -> 0 us
  matrix products: 99.5 us -> 0 us
  other arithmetic: 71.9 us -> 0 us
  local copies, waits for them, and re-layouts: 60.8 us -> 4.84 us
  loops' own time: 15.2 us -> 0 us
  between operations: 13.4 us -> 0.01 us
    pallas_call x0 -> x1, Pallas kernels: none -> 333 us  [on_device(): pl.pallas_call(functools.partial(relay_kernel, micro, sections, replicas)...]
    reduce_scatter x1 -> x0, waiting for transfers between devices: 315 us -> none  [on_device(): lax.psum_scatter(lax.dot_general(normed_all, slope_all, (((0,), (0,)), ((...]
    ppermute x22 -> x0, waiting for transfers between devices: 182 us -> none  [from_behind(): return lax.ppermute(array, axis, pairs)]
    ppermute x22 -> x0, starting transfers between devices: 113 us -> none  [from_behind(): return lax.ppermute(array, axis, pairs)]
    dot_general x9 -> x0, matrix products: 99.5 us -> none  [the longest x4 50.7 us: backward_layer(): lax.dot_general(slope, weight, (((1,), (1,)), ((), ())), preferred_elemen...]
    dynamic_slice x55 -> x0, local copies, waits for them, and re-layouts: 52.9 us -> none  [the longest x11 14.9 us: forward_tick(): old_gate = lax.dynamic_index_in_dim(kept_gates, slot, 0, keepdims=False)]
    dynamic_update_slice x33 -> x0, other arithmetic: 47 us -> none  [the longest x11 23.6 us: forward_tick(): lax.dynamic_update_index_in_dim(kept_inputs, jnp.where(active, source, ol...]
    convert_element_type x8 -> x0, other arithmetic: 16 us -> none  [the longest x4 9.19 us: backward_layer(): (up_float * sigma * (1.0 + gate_value * (1.0 - sigma))).astype(jnp.bfloat16)]
  transfers between devices with their start and end apart: 23 -> 0, of which waited for: 12 -> 0; matrix products, arithmetic and copies ran while one was open for 6% -> 0% of each run, Pallas kernels for 0% -> 0%
where the time goes in v1:
time: 338 us
  Pallas kernels  333 us (99%)
  local copies, waits for them, and re-layouts  4.84 us (1%)
    pallas_call x1, Pallas kernels, on_device(): pl.pallas_call(functools.partial(relay_kernel, micro, sections, replicas)...  333 us

profile of v1, /device:TPU:0, one launch (start us, length us, event | category | flops | bytes accessed | tf_op | source)
XLA Modules:
  0.0 337.7 jit_solution(8406517054116688530)
XLA Ops:
  0.0 332.8 %shard_map.37 = bf16[768,3072]{1,0:T(8,128)(2,1)} custom-call(bf16[384,3072]{1,0:T(8,128)(2,1)} %bitcast.6, bf16[3072,3072]{1,0:T(8,128)(2,1)} %bitcast.5, bf16[384,3072]{1,0:T(8,128)(2,1)} %bitcast.7), custom_call_target="tpu_custom_call" | custom-call | flops 21743271936 | bytes 28311552 | tf_op jit(solution)/shard_map/pallas_call | solution.py:279
  332.8 4.8 %copy.5 = bf16[1,768,3072]{2,1,0:T(8,128)(2,1)} copy(bf16[1,768,3072]{2,1,0:T(8,128)(2,1)} %bitcast.4) | data formatting | bytes 9437184

commit v2 on v1

--- a/solution.py
+++ b/solution.py
@@ -16,7 +16,7 @@
 def relay_kernel(
     micro, sections, replicas,
     in_ref, w_hbm, cot_ref, out_ref,
-    w, xs, acts, gates, ups, slopes, normed, normed_in, normed_t, facs,
+    w, xs, acts, gates, ups, slopes, normed, normed_in, normed_t, facs, sums,
     w_sem, first_sem, cot_sem, act_send, act_recv, down_send, down_recv,
     norm_send, norm_recv, right_send, left_send, slope_recv,
 ):
@@ -113,8 +113,7 @@
     def go_left(origin, m):
         return slope_copy(origin, m, me - 1, left_send)
 
-    @pl.loop(0, micro)
-    def _(m):
+    def forward(m):
         here = rows_of(m)
 
         @pl.when(is_first)
@@ -153,22 +152,16 @@
             def _():
                 act_copy(m, cols).start()
 
-    @pl.when(jnp.logical_not(is_last))
-    def _():
-        @pl.loop(0, micro)
-        def _(m):
+    def backward(m):
+        here = rows_of(m)
+
+        @pl.when(is_last)
+        def _():
+            load_cot(m).wait()
+
+        @pl.when(jnp.logical_not(is_last))
+        def _():
             act_copy(m).wait_send()
-
-    @pl.loop(0, micro)
-    def _(m):
-        here = rows_of(m)
-
-        @pl.when(is_last)
-        def _():
-            load_cot(m).wait()
-
-        @pl.when(jnp.logical_not(is_last))
-        def _():
             down_copy(m).wait_recv()
 
         @pl.loop(0, tiles)
@@ -213,6 +206,18 @@
                 acts[here, cols] = down.astype(jnp.bfloat16)
                 down_copy(m, cols).start()
 
+    lag = jnp.minimum(sections - 1 - section, micro - 1)
+
+    @pl.loop(0, 2 * micro - 1)
+    def _(t):
+        @pl.when(t < micro)
+        def _():
+            forward(t)
+
+        @pl.when(jnp.logical_and(t >= lag, t < lag + micro))
+        def _():
+            backward(t - lag)
+
     for step in range(1, replicas):
         @pl.loop(0, micro)
         def _(m):
@@ -223,6 +228,19 @@
     for origin in range(replicas):
         normed_t[:, pl.ds(origin * tokens, tokens)] = normed_in[origin].T
 
+    def add_origin(origin, start):
+        left = pl.ds(pl.multiple_of(origin * tokens, tokens), tokens)
+
+        @pl.loop(0, width // OUT_TILE)
+        def _(n):
+            cols = pl.ds(pl.multiple_of(n * OUT_TILE, OUT_TILE), OUT_TILE)
+            term = jnp.dot(
+                normed_t[:, left], slopes[origin, :, cols], preferred_element_type=jnp.float32
+            )
+            sums[:, cols] = term if start else sums[:, cols] + term
+
+    add_origin(me, True)
+
     for far in range(1, replicas):
         @pl.loop(0, micro)
         def _(m):
@@ -242,14 +260,20 @@
                 def _():
                     go_left(me + far, m).start()
 
+        @pl.when(me - far >= 0)
+        def _():
+            add_origin(me - far, False)
+
+        @pl.when(me + far < replicas)
+        def _():
+            add_origin(me + far, False)
+
     scale = 1.0 / math.sqrt(tokens * replicas)
 
     @pl.loop(0, width // OUT_TILE)
     def _(n):
         cols = pl.ds(pl.multiple_of(n * OUT_TILE, OUT_TILE), OUT_TILE)
-        right = slopes[:, :, cols].reshape(replicas * tokens, OUT_TILE)
-        total = jnp.dot(normed_t[...], right, preferred_element_type=jnp.float32)
-        out_ref[:, cols] = (total * scale).astype(jnp.bfloat16)
+        out_ref[:, cols] = (sums[:, cols] * scale).astype(jnp.bfloat16)
 
     @pl.loop(0, micro)
     def _(m):
@@ -292,6 +316,7 @@
             pltpu.VMEM((replicas, tokens, chunk), bf16),
             pltpu.VMEM((chunk, replicas * tokens), bf16),
             pltpu.VMEM((tokens, 128), f32),
+            pltpu.VMEM((chunk, width), f32),
             dma, dma((micro,)), dma((micro,)),
             dma((micro,)), dma((micro,)), dma((micro,)), dma((micro,)),
             dma((replicas, micro)), dma((replicas, micro)),

time: 338 us -> 334 us (0.988)
  Pallas kernels: 333 us -> 329 us
    pallas_call x1, Pallas kernels: 333 us -> 329 us  [on_device(): pl.pallas_call(functools.partial(relay_kernel, micro, sections, replicas)...]
where the time goes in v2:
time: 334 us
  Pallas kernels  329 us (99%)
  local copies, waits for them, and re-layouts  4.84 us (1%)
    pallas_call x1, Pallas kernels, on_device(): pl.pallas_call(functools.partial(relay_kernel, micro, sections, replicas)...  329 us

profile of v2, /device:TPU:0, one launch (start us, length us, event | category | flops | bytes accessed | tf_op | source)
XLA Modules:
  0.0 333.5 jit_solution(1692499807525740764)
XLA Ops:
  0.0 328.7 %shard_map.37 = bf16[768,3072]{1,0:T(8,128)(2,1)} custom-call(bf16[384,3072]{1,0:T(8,128)(2,1)} %bitcast.6, bf16[3072,3072]{1,0:T(8,128)(2,1)} %bitcast.5, bf16[384,3072]{1,0:T(8,128)(2,1)} %bitcast.7), custom_call_target="tpu_custom_call" | custom-call | flops 21743271936 | bytes 28311552 | tf_op jit(solution)/shard_map/pallas_call | solution.py:303
  328.7 4.8 %copy.5 = bf16[1,768,3072]{2,1,0:T(8,128)(2,1)} copy(bf16[1,768,3072]{2,1,0:T(8,128)(2,1)} %bitcast.4) | data formatting | bytes 9437184

commit v3 on v2

--- a/solution.py
+++ b/solution.py
@@ -134,16 +134,8 @@
 
         @pl.loop(0, tiles)
         def _(n):
-            part = xs[here, cols_of(n)].astype(jnp.float32)
-            normed[here, cols_of(n)] = (part * fac).astype(jnp.bfloat16)
-
-        for step in range(1, replicas):
-            norm_copy(m, step).start()
-
-        @pl.loop(0, tiles)
-        def _(n):
             cols = cols_of(n)
-            gate = jnp.dot(normed[here, :], w[:, cols], preferred_element_type=jnp.float32)
+            gate = fac * jnp.dot(xs[here, :], w[:, cols], preferred_element_type=jnp.float32)
             gates[here, cols] = gate
             out = xs[here, cols].astype(jnp.float32) + gate / (1.0 + jnp.exp(-gate))
             acts[here, cols] = out.astype(jnp.bfloat16)
@@ -152,6 +144,14 @@
             def _():
                 act_copy(m, cols).start()
 
+        @pl.loop(0, tiles)
+        def _(n):
+            part = xs[here, cols_of(n)].astype(jnp.float32)
+            normed[here, cols_of(n)] = (part * fac).astype(jnp.bfloat16)
+
+        for step in range(1, replicas):
+            norm_copy(m, step).start()
+
     def backward(m):
         here = rows_of(m)
 
@@ -164,14 +164,17 @@
             act_copy(m).wait_send()
             down_copy(m).wait_recv()
 
-        @pl.loop(0, tiles)
-        def _(n):
+        def slope_tile(n, total):
             cols = cols_of(n)
             gate = gates[here, cols]
             sig = 1.0 / (1.0 + jnp.exp(-gate))
             up = ups[here, cols].astype(jnp.float32)
-            slope = up * sig * (1.0 + gate * (1.0 - sig))
-            slopes[me, here, cols] = slope.astype(jnp.bfloat16)
+            slope = (up * sig * (1.0 + gate * (1.0 - sig))).astype(jnp.bfloat16)
+            slopes[me, here, cols] = slope
+            return total + jnp.sum(slope.astype(jnp.float32) * gate, axis=-1, keepdims=True)
+
+        total = lax.fori_loop(0, tiles, slope_tile, jnp.zeros((rows, 1), jnp.float32))
+        mean = total / width
 
         @pl.when(me < replicas - 1)
         def _():
@@ -185,24 +188,15 @@
 
         @pl.when(jnp.logical_not(is_first))
         def _():
-            def back_tile(n, total):
+            @pl.loop(0, tiles)
+            def _(n):
                 cols = cols_of(n)
                 back = lax.dot_general(
                     slopes[me, here, :], w[cols, :], (((1,), (1,)), ((), ())),
                     preferred_element_type=jnp.float32,
                 )
-                gates[here, cols] = back
                 unit = xs[here, cols].astype(jnp.float32) * fac
-                return total + jnp.sum(back * unit, axis=-1, keepdims=True)
-
-            total = lax.fori_loop(0, tiles, back_tile, jnp.zeros((rows, 1), jnp.float32))
-            mean = total / width
-
-            @pl.loop(0, tiles)
-            def _(n):
-                cols = cols_of(n)
-                unit = xs[here, cols].astype(jnp.float32) * fac
-                down = ups[here, cols].astype(jnp.float32) + fac * (gates[here, cols] - unit * mean)
+                down = ups[here, cols].astype(jnp.float32) + fac * (back - unit * mean)
                 acts[here, cols] = down.astype(jnp.bfloat16)
                 down_copy(m, cols).start()
 

time: 334 us -> 312 us (0.934)
  Pallas kernels: 329 us -> 307 us
    pallas_call x1, Pallas kernels: 329 us -> 307 us  [on_device(): pl.pallas_call(functools.partial(relay_kernel, micro, sections, replicas)...]
where the time goes in v3:
time: 312 us
  Pallas kernels  307 us (98%)
  local copies, waits for them, and re-layouts  4.84 us (2%)
    pallas_call x1, Pallas kernels, on_device(): pl.pallas_call(functools.partial(relay_kernel, micro, sections, replicas)...  307 us

profile of v3, /device:TPU:0, one launch (start us, length us, event | category | flops | bytes accessed | tf_op | source)
XLA Modules:
  0.0 312.0 jit_solution(7786367473874938638)
XLA Ops:
  0.0 307.1 %shard_map.37 = bf16[768,3072]{1,0:T(8,128)(2,1)} custom-call(bf16[384,3072]{1,0:T(8,128)(2,1)} %bitcast.6, bf16[3072,3072]{1,0:T(8,128)(2,1)} %bitcast.5, bf16[384,3072]{1,0:T(8,128)(2,1)} %bitcast.7), custom_call_target="tpu_custom_call" | custom-call | flops 21743271936 | bytes 28311552 | tf_op jit(solution)/shard_map/pallas_call | solution.py:297
  307.1 4.8 %copy.5 = bf16[1,768,3072]{2,1,0:T(8,128)(2,1)} copy(bf16[1,768,3072]{2,1,0:T(8,128)(2,1)} %bitcast.4) | data formatting | bytes 9437184
